TPU v7x, 512 devices: a whole 4x4x16 slice. The times are simulated.
512 devices in a mesh: fsdp: 32 (over z, core), rep: 16 (over y, x).
Axes of the slice: x: 4, y: 4, z: 16, core: 2. Of those that a mesh axis runs over, the one named last changes fastest.
Arguments:
- grads: bfloat16 [96, 16, 64, 1024], P(None, 'rep', 'fsdp'), may hold values from -4 to 4
- assignment: int32 [96], replicated, may hold values from 0 to 95, each once
- extents: int32 [96, 2], replicated, may hold values from 256 to 1024, as said below
- factor_left: float32 [96, 1024, 1024], P('fsdp', 'rep')
- factor_right: float32 [96, 1024, 1024], P('fsdp', 'rep')
- root_left: bfloat16 [96, 1024, 1024], P('fsdp', 'rep'), as said below
- root_right: bfloat16 [96, 1024, 1024], P('fsdp', 'rep'), as said below
Outputs:
- update: bfloat16 [96, 16, 64, 1024], P(None, 'rep', 'fsdp')
- new_left: float32 [96, 1024, 1024], P('fsdp', 'rep')
- new_right: float32 [96, 1024, 1024], P('fsdp', 'rep')
Inputs may be any that keep to these rules, and one draw needn't show every extreme that they name: `assignment`: each block stands in exactly one owner slot. `extents`: block 0 is full; the last block is cut in its rows; other blocks are full or cut at the edge. Each block of root_right is symmetric. Each block of root_left is symmetric.
All inputs are finite; a program needn't handle non-finite values.
Results may differ from a plain program's by a relative error of at most 0.0049.
Values may be sent and summed in bfloat16 or wider, within the bound.
A program may use at most 64 MiB of HBM per device.

v0:
```python
import jax
import jax.numpy as jnp
from jax import lax
from jax.sharding import PartitionSpec as P

BETA = 0.95


def factor_terms(gathered, own_rows, left, right, root_r, row_start, row_count):
    left_term = jnp.einsum("kid,kjd->kij", own_rows, gathered, preferred_element_type=jnp.float32)
    col_slice = lax.dynamic_slice_in_dim(gathered, row_start, row_count, 2)
    right_term = jnp.einsum("kdi,kdj->kij", col_slice, gathered, preferred_element_type=jnp.float32)
    next_left = BETA * left + (1.0 - BETA) * left_term
    next_right = BETA * right + (1.0 - BETA) * right_term
    precond_part = jnp.einsum("kad,kid->kai", gathered, root_r, preferred_element_type=jnp.float32)
    return (next_left, next_right, precond_part.astype(jnp.bfloat16))


def local(grads, assignment, extents, factor_left, factor_right, root_left, root_right):
    owned_slots = factor_left.shape[0]
    row_count = factor_left.shape[1]
    width = factor_left.shape[2]
    nblocks = assignment.shape[0]
    row_start = lax.axis_index("rep") * row_count
    ordered = jnp.take(grads, assignment, axis=0)
    received = lax.all_to_all(ordered, "fsdp", split_axis=0, concat_axis=2, tiled=True)
    own_rows = received.reshape(owned_slots, row_count, width)
    first_slot = lax.axis_index("fsdp") * owned_slots
    slot_ids = lax.dynamic_slice_in_dim(assignment, first_slot, owned_slots, 0)
    slot_ext = jnp.take(extents, slot_ids, axis=0)
    row_ids = row_start + jnp.arange(row_count, dtype=jnp.int32)
    col_ids = jnp.arange(width, dtype=jnp.int32)
    row_valid = row_ids[None, :] < slot_ext[:, 0:1]
    col_valid = col_ids[None, :] < slot_ext[:, 1:2]
    valid = row_valid[:, :, None] & col_valid[:, None, :]
    own_rows = jnp.where(valid, own_rows, jnp.zeros_like(own_rows))
    left_list = []
    right_list = []
    update_list = []
    for slot in range(owned_slots):
        piece_rows = own_rows[slot : slot + 1]
        gathered = lax.all_gather(piece_rows, "rep", axis=1, tiled=True)
        next_left, next_right, precond_part = factor_terms(
            gathered,
            piece_rows,
            factor_left[slot : slot + 1],
            factor_right[slot : slot + 1],
            root_right[slot : slot + 1],
            row_start,
            row_count,
        )
        precond_full = lax.all_gather(precond_part, "rep", axis=2, tiled=True)
        update_list.append(
            jnp.einsum(
                "kid,kdj->kij",
                root_left[slot : slot + 1],
                precond_full,
                preferred_element_type=jnp.float32,
            )
        )
        left_list.append(next_left)
        right_list.append(next_right)
    new_left = jnp.concatenate(left_list, axis=0)
    new_right = jnp.concatenate(right_list, axis=0)
    slot_update = jnp.concatenate(update_list, axis=0)
    slot_update = jnp.where(valid, slot_update, jnp.zeros_like(slot_update)).astype(jnp.bfloat16)
    returned = lax.all_to_all(
        slot_update.reshape(owned_slots, 1, row_count, width),
        "fsdp",
        split_axis=2,
        concat_axis=0,
        tiled=True,
    )
    block_line = jnp.arange(nblocks, dtype=jnp.int32)
    inverse = jnp.sum(
        jnp.where(assignment[None, :] == block_line[:, None], block_line[None, :], 0), axis=1
    )
    update = jnp.take(returned, inverse, axis=0)
    return (update, new_left, new_right)


def solution(mesh):
    placed = (
        P(None, "rep", "fsdp", None),
        P(),
        P(),
        P("fsdp", "rep", None),
        P("fsdp", "rep", None),
        P("fsdp", "rep", None),
        P("fsdp", "rep", None),
    )
    return jax.shard_map(
        local,
        mesh=mesh,
        in_specs=placed,
        out_specs=(P(None, "rep", "fsdp", None), P("fsdp", "rep", None), P("fsdp", "rep", None)),
        check_vma=False,
    )
```

profile of v0, /device:TPU:1, one launch (start us, length us, event | category | flops | bytes accessed | tf_op | source)
XLA Modules:
  0.0 484.9 jit_solution(15434940803986406385)
XLA Ops:
  7.2 0.7 compare_select_fusion.1
  7.9 0.7 compare_and_fusion.1
  8.6 1.4 gather_fusion.1
  10.0 1.2 broadcast_select_fusion.1
  11.2 16.9 %all-to-all-start = ((bf16[96,1,2,1024]{3,2,1,0:T(2,128)(2,1)}), bf16[96,1,2,1024]{3,2,1,0:T(2,128)(2,1)S(1)}, u32[]{:S(2)}, u32[]{:S(2)}) async-start(bf16[96,1,2,1024]{3,2,1,0:T(2,128)(2,1)} %broadcast_select_fusion.1), calls=%async_computation | async-start | bytes 786432 | tf_op jit(solution)/shard_map/all_to_all | solution.py:26
  28.1 0.1 copy.32
  28.2 0.1 compare_and_fusion.2
  28.3 0.6 gather_fusion
  28.9 0.2 slice_reduce_fusion.1
  29.1 0.1 broadcast_compare_fusion
  29.2 0.1 iota_compare_fusion.1
  29.3 26.7 %all-to-all-done = bf16[96,1,2,1024]{3,2,1,0:T(2,128)(2,1)S(1)} async-done(((bf16[96,1,2,1024]{3,2,1,0:T(2,128)(2,1)}), bf16[96,1,2,1024]{3,2,1,0:T(2,128)(2,1)S(1)}, u32[]{:S(2)}, u32[]{:S(2)}) %all-to-all-start) | async-done | bytes 393248 | tf_op jit(solution)/shard_map/all_to_all | solution.py:26
  56.0 0.3 copy.42
  56.3 0.1 reshape.213
  56.5 0.2 and_select_fusion
  56.6 0.8 fusion.110
  57.5 0.7 all-gather.12.cloned.1.call-update
  58.2 0.7 all-gather.10.cloned.1.call-update
  59.0 49.3 %all-gather.14.cloned.1.call-done = bf16[1,1024,1024]{2,1,0:T(8,128)(2,1)} async-done(((bf16[1,64,1024]{2,1,0:T(8,128)(2,1)}), bf16[1,1024,1024]{2,1,0:T(8,128)(2,1)}) %all-gather.14.cloned.1.call-update) | async-done | bytes 2097168 | tf_op jit(solution)/shard_map/all_gather | solution.py:42
  108.2 3.0 fusion.78
  111.3 60.2 %all-gather.12.cloned.1.call-done = bf16[1,1024,1024]{2,1,0:T(8,128)(2,1)} async-done(((bf16[1,64,1024]{2,1,0:T(8,128)(2,1)}), bf16[1,1024,1024]{2,1,0:T(8,128)(2,1)}) %all-gather.12.cloned.1.call-update) | async-done | bytes 2097168 | tf_op jit(solution)/shard_map/all_gather | solution.py:42
  171.6 3.0 fusion.75
  174.6 60.2 %all-gather.10.cloned.1.call-done = bf16[1,1024,1024]{2,1,0:T(8,128)(2,1)} async-done(((bf16[1,64,1024]{2,1,0:T(8,128)(2,1)}), bf16[1,1024,1024]{2,1,0:T(8,128)(2,1)}) %all-gather.10.cloned.1.call-update) | async-done | bytes 2097168 | tf_op jit(solution)/shard_map/all_gather | solution.py:42
  234.9 3.0 fusion.72
  237.9 0.1 select_reduce_fusion
  238.1 2.3 fusion.54
  240.4 57.7 %all-gather.20.cloned.1.call-done = bf16[1024,1024]{0,1:T(8,128)(2,1)} async-done(((bf16[1024,64]{0,1:T(8,128)(2,1)}), bf16[1024,1024]{0,1:T(8,128)(2,1)}) %all-gather.20.cloned.1.call-update) | async-done | bytes 2097168 | tf_op jit(solution)/shard_map/all_gather | solution.py:52
  298.1 2.3 convolution_bitcast_fusion
  300.4 60.8 %all-gather.18.cloned.1.call-done = bf16[1024,1024]{0,1:T(8,128)(2,1)} async-done(((bf16[1024,64]{0,1:T(8,128)(2,1)}), bf16[1024,1024]{0,1:T(8,128)(2,1)}) %all-gather.18.cloned.1.call-update) | async-done | bytes 2097168 | tf_op jit(solution)/shard_map/all_gather | solution.py:52
  361.2 2.3 convolution_bitcast_fusion.1
  363.6 60.3 %all-gather.16.cloned.1.call-done = bf16[1024,1024]{0,1:T(8,128)(2,1)} async-done(((bf16[1024,64]{0,1:T(8,128)(2,1)}), bf16[1024,1024]{0,1:T(8,128)(2,1)}) %all-gather.16.cloned.1.call-update) | async-done | bytes 2097168 | tf_op jit(solution)/shard_map/all_gather | solution.py:52
  423.9 2.3 convolution_bitcast_fusion.2
  426.2 0.2 fusion.81
  426.4 1.1 copy.34
  427.5 13.8 %all-to-all-start.1 = ((bf16[3,1,64,1024]{3,0,1,2:T(4,128)(2,1)}), bf16[3,1,64,1024]{3,0,1,2:T(4,128)(2,1)S(1)}, u32[]{:S(2)}, u32[]{:S(2)}) async-start(bf16[3,1,64,1024]{3,0,1,2:T(4,128)(2,1)} %copy.34), calls=%async_computation.1 | async-start | bytes 1048576 | tf_op jit(solution)/shard_map/all_to_all | solution.py:67
  441.4 2.4 fusion.60
  443.9 1.7 fusion.66
  445.6 1.0 pad_maximum_fusion.1
  446.5 0.8 fusion.57
  447.3 0.1 copy-done.2
  447.4 0.8 fusion.63
  448.2 0.8 fusion.69
  449.0 1.0 pad_maximum_fusion
  449.9 25.0 %all-to-all-done.1 = bf16[3,1,64,1024]{3,0,1,2:T(4,128)(2,1)S(1)} async-done(((bf16[3,1,64,1024]{3,0,1,2:T(4,128)(2,1)}), bf16[3,1,64,1024]{3,0,1,2:T(4,128)(2,1)S(1)}, u32[]{:S(2)}, u32[]{:S(2)}) %all-to-all-start.1) | async-done | bytes 393248 | tf_op jit(solution)/shard_map/all_to_all | solution.py:67
  474.9 0.3 copy.41
  475.2 0.3 copy.36
  475.5 1.4 gather_fusion.2
  476.9 1.2 fusion.82
  (36 shorter events, 0.5 us)
Async XLA Ops:
  7.2 1.4 copy-start
  7.2 21.0 %copy-start.9 = (s32[96]{0:T(128)S(1)}, s32[96]{0:T(128)}, u32[]{:S(2)}) copy-start(s32[96]{0:T(128)} %param.10) | copy-start | bytes 1156
  7.2 20.9 %copy-start.8 = (s32[96,2]{0,1:T(2,128)S(1)}, s32[96,2]{0,1:T(2,128)}, u32[]{:S(2)}) copy-start(s32[96,2]{0,1:T(2,128)} %param.11) | copy-start | bytes 2308
  11.1 97.1 %copy-start.6 = (bf16[3,64,1024]{2,1,0:T(8,128)(2,1)S(1)}, bf16[3,64,1024]{2,1,0:T(8,128)(2,1)}, u32[]{:S(2)}) copy-start(bf16[3,64,1024]{2,1,0:T(8,128)(2,1)} %param.15) | copy-start | bytes 1179652
  11.2 44.9 %all-to-all-start = ((bf16[96,1,2,1024]{3,2,1,0:T(2,128)(2,1)}), bf16[96,1,2,1024]{3,2,1,0:T(2,128)(2,1)S(1)}, u32[]{:S(2)}, u32[]{:S(2)}) async-start(bf16[96,1,2,1024]{3,2,1,0:T(2,128)(2,1)} %broadcast_select_fusion.1), calls=%async_computation | async-start | bytes 786432 | tf_op jit(solution)/shard_map/all_to_all | solution.py:26
  28.0 80.2 %all-gather.14.cloned.1.call-start = ((), (), s32[]{:S(2)}) async-start(), calls=%async_computation.4 | async-start | bytes 2228224 | tf_op jit(solution)/shard_map/all_gather | solution.py:42
  57.4 114.1 %all-gather.12.cloned.1.call-start = ((), (), s32[]{:S(2)}) async-start(), calls=%async_computation.3 | async-start | bytes 2228224 | tf_op jit(solution)/shard_map/all_gather | solution.py:42
  58.2 176.7 %all-gather.10.cloned.1.call-start = ((), (), s32[]{:S(2)}) async-start(), calls=%async_computation.2 | async-start | bytes 2228224 | tf_op jit(solution)/shard_map/all_gather | solution.py:42
  58.9 239.2 %all-gather.20.cloned.1.call-start = ((), (), s32[]{:S(2)}) async-start(), calls=%async_computation.7 | async-start | bytes 2228224 | tf_op jit(solution)/shard_map/all_gather | solution.py:52
  111.3 126.8 %copy-start.1 = (bf16[1,1024,1024]{2,1,0:T(8,128)(2,1)S(1)}, bf16[1,1024,1024]{2,1,0:T(8,128)(2,1)}, u32[]{:S(2)}) copy-start(bf16[1,1024,1024]{2,1,0:T(8,128)(2,1)} %all-gather.14.cloned.1.call-done) | copy-start | bytes 6291460
  111.3 250.0 %all-gather.18.cloned.1.call-start = ((), (), s32[]{:S(2)}) async-start(), calls=%async_computation.6 | async-start | bytes 2228224 | tf_op jit(solution)/shard_map/all_gather | solution.py:52
  174.6 249.3 %all-gather.16.cloned.1.call-start = ((), (), s32[]{:S(2)}) async-start(), calls=%async_computation.5 | async-start | bytes 2228224 | tf_op jit(solution)/shard_map/all_gather | solution.py:52
  237.9 60.2 %copy-start.7 = (bf16[3,64,1024]{2,1,0:T(8,128)(2,1)S(1)}, bf16[3,64,1024]{2,1,0:T(8,128)(2,1)}, u32[]{:S(2)}) copy-start(bf16[3,64,1024]{2,1,0:T(8,128)(2,1)} %param.14) | copy-start | bytes 1179652
  427.5 47.4 %all-to-all-start.1 = ((bf16[3,1,64,1024]{3,0,1,2:T(4,128)(2,1)}), bf16[3,1,64,1024]{3,0,1,2:T(4,128)(2,1)S(1)}, u32[]{:S(2)}, u32[]{:S(2)}) async-start(bf16[3,1,64,1024]{3,0,1,2:T(4,128)(2,1)} %copy.34), calls=%async_computation.1 | async-start | bytes 1048576 | tf_op jit(solution)/shard_map/all_to_all | solution.py:67
  441.4 2.5 copy-start.3
  441.4 4.2 copy-start.4
  443.9 2.7 copy-start.5
  445.6 1.9 copy-start.2
Sparse Core Ops, SparseCore 0:
  57.5 50.6 all-gather.13
  111.8 59.6 all-gather.11
  175.1 59.6 all-gather.9
  238.3 59.6 all-gather.19
  301.5 59.6 all-gather.17
  364.1 59.6 all-gather.15
where the time goes:
time: 485 us
  waiting for transfers between devices  402 us (83%)
  starting transfers between devices  31 us (6%)
  matrix products  24.8 us (5%)
  between operations  14.4 us (3%)
  local copies, waits for them, and re-layouts  6.67 us (1%)
  other arithmetic  6.49 us (1%)
    all_gather x3, waiting for transfers between devices, local(): precond_full = lax.all_gather(precond_part, 'rep', axis=2, tiled=True)  179 us
    all_gather x3, waiting for transfers between devices, local(): gathered = lax.all_gather(piece_rows, 'rep', axis=1, tiled=True)  170 us
    all_to_all x1, waiting for transfers between devices, local(): lax.all_to_all(ordered, 'fsdp', split_axis=0, concat_axis=2, tiled=True)  26.7 us
    all_to_all x1, waiting for transfers between devices, local(): lax.all_to_all(slot_update.reshape(owned_slots, 1, row_count, width), 'fs...  25 us
    all_to_all x1, starting transfers between devices, local(): lax.all_to_all(ordered, 'fsdp', split_axis=0, concat_axis=2, tiled=True)  16.9 us
    all_to_all x1, starting transfers between devices, local(): lax.all_to_all(slot_update.reshape(owned_slots, 1, row_count, width), 'fs...  13.8 us
  transfers between devices with their start and end apart: 8, of which 8 were waited for; matrix products, arithmetic and copies ran while one was open for 5% of the time, Pallas kernels for 0%

commit v1 on v0

v1 whole, which is shorter than its diff:
```python
import functools

import jax
import jax.numpy as jnp
from jax import lax
from jax.experimental import pallas as pl
from jax.experimental.pallas import tpu as pltpu
from jax.sharding import PartitionSpec as P

BETA = 0.95
MESH = pl.DeviceIdType.MESH
SIDE = 4
SLOTS = 3
RW = 64
BS = 1024
LANES = 128
F32 = jnp.float32
BF16 = jnp.bfloat16


def kernel(
    nf, tiles, asg, ext, root_l, root_r, ret, left_out, right_out,
    zin, fold_in, g_full, r_full, l_own, g_own, t_buf, u_buf, u_tiles, u_in, left_buf, right_buf, acc, perm, perm_t,
    z_send, z_recv, gf_send, gf_recv, rf_send, rf_recv, lf_send, lf_recv,
    ga_send, ga_recv, ra_send, ra_recv, u_send, u_recv, lo_send, lo_recv, ro_send, ro_recv, b_send, b_recv,
):
    tile_rows = tiles.shape[2]
    rpf = RW // nf
    me = lax.axis_index("fsdp")
    rep = lax.axis_index("rep")
    core = lax.rem(me, 2)
    y, x = rep // SIDE, lax.rem(rep, SIDE)
    fold = jnp.where(core == 0, y, x)
    ring = jnp.where(core == 0, x, y)
    fold_step = jnp.where(core == 0, SIDE, 1)
    ring_step = jnp.where(core == 0, 1, SIDE)

    def at(fold_pos, ring_pos):
        return fold_pos * fold_step + ring_pos * ring_step

    right = lax.rem(ring + 1, SIDE)
    left = lax.rem(ring + SIDE - 1, SIDE)
    across = lax.rem(ring + 2, SIDE)
    works = fold < SLOTS

    def remote(src, dst, ssem, rsem, fs, rp):
        return pltpu.make_async_remote_copy(
            src_ref=src, dst_ref=dst, send_sem=ssem, recv_sem=rsem, device_id=(fs, rp), device_id_type=MESH
        )

    def taken(ref, sem):
        pltpu.make_async_copy(ref, ref, sem).wait()

    barrier = pltpu.get_barrier_semaphore()

    def greet(d, carry):
        pl.semaphore_signal(barrier, inc=1, device_id=(lax.rem(me + d, nf), rep), device_id_type=MESH)
        return carry

    lax.fori_loop(1, nf, greet, 0)
    for d in range(1, SIDE):
        pl.semaphore_signal(barrier, inc=1, device_id=(me, at(lax.rem(fold + d, SIDE), ring)), device_id_type=MESH)
    for pos in (left, right):
        pl.semaphore_signal(barrier, inc=1, device_id=(me, at(fold, pos)), device_id_type=MESH)
    pl.semaphore_wait(barrier, nf - 1 + SIDE - 1 + 2)

    for s in range(SLOTS):
        @pl.when(fold != s)
        def _():
            remote(root_r.at[s], r_full.at[rep], rf_send.at[s], rf_recv.at[fold], me, at(s, ring)).start()
            remote(root_l.at[s], l_own.at[fold], lf_send.at[s], lf_recv.at[fold], me, at(s, ring)).start()

        @pl.when(fold == s)
        def _():
            pltpu.make_async_copy(root_r.at[s], r_full.at[rep], rf_recv.at[fold]).start()
            pltpu.make_async_copy(root_l.at[s], l_own.at[fold], lf_recv.at[fold]).start()

    def other(i):
        half = (i + 1) // 2
        return lax.rem(me + jnp.where(lax.rem(i, 2) == 1, half, nf - half), nf)

    for s in range(SLOTS):
        pltpu.make_async_copy(tiles.at[s, me], zin.at[s, me], z_recv.at[s]).start()

        def push(i, carry):
            to = other(i)
            remote(tiles.at[s, to], zin.at[s, me], z_send.at[s], z_recv.at[s], to, rep).start()
            return carry

        lax.fori_loop(1, nf, push, 0)

    size = 8 * RW
    one = lax.broadcasted_iota(jnp.int32, (size, size), 0)
    two = lax.broadcasted_iota(jnp.int32, (size, size), 1)

    def tile_place(o):
        return (lax.rem(o, RW) // rpf) * tile_rows + (o // RW) * rpf + lax.rem(o, rpf)

    perm[...] = jnp.where(two == tile_place(one), 1.0, 0.0).astype(BF16)
    perm_t[...] = jnp.where(one == tile_place(two), 1.0, 0.0).astype(BF16)

    def spread(buf, sends, recvs, f):
        g = at(f, ring)
        remote(buf.at[g], buf.at[g], sends.at[0, f], recvs.at[0, f], me, at(fold, right)).start()
        remote(buf.at[g], buf.at[g], sends.at[1, f], recvs.at[1, f], me, at(fold, left)).start()

    def pass_on(buf, sends, recvs):
        for f in range(SIDE):
            way = 0 if f < 2 else 1
            g = at(f, left if way == 0 else right)
            taken(buf.at[g], recvs.at[way, f])
            remote(buf.at[g], buf.at[g], sends.at[2, f], recvs.at[2, f], me, at(fold, right if way == 0 else left)).start()

    def rest(buf, recvs):
        for f in range(SIDE):
            way = 1 if f < 2 else 0
            taken(buf.at[at(f, right if way == 1 else left)], recvs.at[way, f])
            taken(buf.at[at(f, across)], recvs.at[2, f])

    @pl.when(works)
    def _():
        for f in range(SIDE):
            taken(r_full.at[at(f, ring)], rf_recv.at[f])
            spread(r_full, ra_send, ra_recv, f)

    slot = me * SLOTS + jnp.minimum(fold, SLOTS - 1)
    block = asg[slot]
    rows_ok = ext[2 * block]
    cols_ok = ext[2 * block + 1]

    def unpack(i, carry):
        f = lax.rem(fold + i, SIDE)
        taken(fold_in.at[f], gf_recv.at[f])
        g = at(f, ring)
        flat = jnp.dot(perm[...], fold_in[f].reshape(size, LANES), preferred_element_type=F32)
        row_ids = g * RW + lax.broadcasted_iota(jnp.int32, (RW, LANES), 0)
        col_ids = lax.broadcasted_iota(jnp.int32, (RW, LANES), 1)
        for c in range(BS // LANES):
            ok = jnp.logical_and(row_ids < rows_ok, col_ids + c * LANES < cols_ok)
            part = jnp.where(ok, flat[c * RW : (c + 1) * RW, :], 0.0).astype(BF16)
            g_full[g, :, c * LANES : (c + 1) * LANES] = part
            g_own[f, :, c * LANES : (c + 1) * LANES] = part
        spread(g_full, ga_send, ga_recv, f)
        return carry

    for s in range(SLOTS):
        taken(zin.at[s], z_recv.at[s])

        @pl.when(fold != s)
        def _():
            remote(zin.at[s], fold_in.at[fold], gf_send.at[s], gf_recv.at[fold], me, at(s, ring)).start()

        @pl.when(fold == s)
        def _():
            pltpu.make_async_copy(zin.at[s], fold_in.at[fold], gf_recv.at[fold]).start()
            lax.fori_loop(0, SIDE, unpack, 0)

        if s == 0:
            @pl.when(works)
            def _():
                pass_on(r_full, ra_send, ra_recv)
        else:
            @pl.when(fold == s - 1)
            def _():
                pass_on(g_full, ga_send, ga_recv)

    @pl.when(fold == SLOTS - 1)
    def _():
        pass_on(g_full, ga_send, ga_recv)

    width = 256
    own_rows = SIDE * RW

    def columns(j):
        return pl.ds(pl.multiple_of(j * width, width), width)

    def update_part():
        rest(g_full, ga_recv)
        for f in range(SIDE):
            taken(l_own.at[f], lf_recv.at[f])

        def t_cols(j, carry):
            t_buf[:, columns(j)] = jnp.dot(
                l_own[...].reshape(own_rows, BS), g_full[:, :, columns(j)].reshape(BS, width), preferred_element_type=F32
            ).astype(BF16)
            return carry

        lax.fori_loop(0, BS // width, t_cols, 0)
        rest(r_full, ra_recv)

        def u_cols(j, carry):
            u = jnp.dot(t_buf[...], r_full[:, :, columns(j)].reshape(BS, width), preferred_element_type=F32)
            col_ids = j * width + lax.broadcasted_iota(jnp.int32, (RW, width), 1)
            for f in range(SIDE):
                row_ids = at(f, ring) * RW + lax.broadcasted_iota(jnp.int32, (RW, width), 0)
                ok = jnp.logical_and(row_ids < rows_ok, col_ids < cols_ok)
                u_buf[f * RW : (f + 1) * RW, columns(j)] = jnp.where(ok, u[f * RW : (f + 1) * RW, :], 0.0).astype(BF16)
            return carry

        lax.fori_loop(0, BS // width, u_cols, 0)
        for f in range(SIDE):
            rows = u_buf[f * RW : (f + 1) * RW, :]
            flat = jnp.concatenate([rows[:, c * LANES : (c + 1) * LANES] for c in range(BS // LANES)], axis=0)
            u_tiles[f] = (
                jnp.dot(perm_t[...], flat, preferred_element_type=F32).astype(BF16).reshape(nf, tile_rows, LANES)
            )

            @pl.when(fold != f)
            def _():
                remote(u_tiles.at[f], u_in.at[fold], u_send.at[f], u_recv.at[fold], me, at(f, ring)).start()

            @pl.when(fold == f)
            def _():
                pltpu.make_async_copy(u_tiles.at[f], u_in.at[fold], u_recv.at[fold]).start()

    def factor_part():
        def left_cols(j, carry):
            part = lax.dot_general(
                g_own[...].reshape(own_rows, BS),
                g_full[pl.ds(j * (width // RW), width // RW)].reshape(width, BS),
                (((1,), (1,)), ((), ())),
                preferred_element_type=F32,
            )
            left_buf[:, :, columns(j)] = ((1.0 - BETA) * part).astype(BF16).reshape(SIDE, RW, width)
            return carry

        lax.fori_loop(0, BS // width, left_cols, 0)

        def home(buf, out, sends, recvs, f):
            @pl.when(fold != f)
            def _():
                remote(buf.at[f], out.at[fold], sends.at[f], recvs.at[fold], me, at(f, ring)).start()

            @pl.when(fold == f)
            def _():
                pltpu.make_async_copy(buf.at[f], out.at[fold], recvs.at[fold]).start()

        for f in range(SIDE):
            home(left_buf, left_out, lo_send, lo_recv, f)

        for f in range(SIDE):
            g = at(f, ring)
            pair = pl.ds(pl.multiple_of((g // 2) * LANES, LANES), LANES)

            def right_cols(j, carry):
                acc[...] = lax.dot_general(
                    g_full[:, :, pair].reshape(BS, LANES),
                    g_full[:, :, columns(j)].reshape(BS, width),
                    (((0,), (0,)), ((), ())),
                    preferred_element_type=F32,
                )
                mine = acc[pl.ds(pl.multiple_of(lax.rem(g, 2) * RW, RW), RW), :]
                right_buf[f, :, columns(j)] = ((1.0 - BETA) * mine).astype(BF16)
                return carry

            lax.fori_loop(0, BS // width, right_cols, 0)
            home(right_buf, right_out, ro_send, ro_recv, f)

    for s in range(SLOTS):
        pl.when(fold == s)(update_part)
        taken(u_in.at[s], u_recv.at[s])
        pltpu.make_async_copy(u_in.at[s, me], ret.at[s, me], b_recv.at[s]).start()

        def push_back(i, carry):
            to = other(i)
            remote(u_in.at[s, to], ret.at[s, me], b_send.at[s], b_recv.at[s], to, rep).start()
            return carry

        lax.fori_loop(1, nf, push_back, 0)
        pl.when(fold == s)(factor_part)

    for s in range(SLOTS):
        taken(left_out.at[s], lo_recv.at[s])
        taken(right_out.at[s], ro_recv.at[s])
        taken(ret.at[s], b_recv.at[s])
        taken(zin.at[s, pl.ds(0, nf - 1)], z_send.at[s])
        taken(u_in.at[s, pl.ds(0, nf - 1)], b_send.at[s])

        @pl.when(fold != s)
        def _():
            taken(zin.at[s], gf_send.at[s])
            taken(root_r.at[s], rf_send.at[s])
            taken(root_l.at[s], lf_send.at[s])

    @pl.when(works)
    def _():
        for f in range(SIDE):
            for way in range(3):
                taken(g_full.at[f], ga_send.at[way, f])
                taken(r_full.at[f], ra_send.at[way, f])

            @pl.when(fold != f)
            def _():
                taken(u_tiles.at[f], u_send.at[f])
                taken(left_buf.at[f], lo_send.at[f])
                taken(right_buf.at[f], ro_send.at[f])


def local(nf, grads, assignment, extents, factor_left, factor_right, root_left, root_right):
    nblocks = assignment.shape[0]
    rpf = RW // nf
    tile_rows = rpf * BS // LANES
    by_slot = assignment.reshape(nf, SLOTS).T.reshape(-1)
    ordered = grads.reshape(nblocks, rpf, BS).at[by_slot].get(mode="promise_in_bounds")
    tiles = ordered.reshape(nblocks, rpf, BS // LANES, LANES).transpose(0, 2, 1, 3)
    tiles = tiles.reshape(SLOTS, nf, tile_rows, LANES)
    dma = pltpu.SemaphoreType.DMA
    anywhere = pl.BlockSpec(memory_space=pl.ANY)
    vmem = pl.BlockSpec(memory_space=pltpu.VMEM)
    smem = pl.BlockSpec(memory_space=pltpu.SMEM)
    rows = (SLOTS, RW, BS)
    own = (SIDE, RW, BS)
    ret, left_term, right_term = pl.pallas_call(
        functools.partial(kernel, nf),
        out_shape=(
            jax.ShapeDtypeStruct((SLOTS, nf, tile_rows, LANES), BF16),
            jax.ShapeDtypeStruct(rows, BF16),
            jax.ShapeDtypeStruct(rows, BF16),
        ),
        in_specs=[vmem, smem, smem, anywhere, anywhere],
        out_specs=(anywhere, anywhere, anywhere),
        scratch_shapes=[
            pltpu.VMEM((SLOTS, nf, tile_rows, LANES), BF16),
            pltpu.VMEM((SIDE, nf, tile_rows, LANES), BF16),
            pltpu.VMEM((SIDE * SIDE, RW, BS), BF16),
            pltpu.VMEM((SIDE * SIDE, RW, BS), BF16),
            pltpu.VMEM(own, BF16),
            pltpu.VMEM(own, BF16),
            pltpu.VMEM((SIDE * RW, BS), BF16),
            pltpu.VMEM((SIDE * RW, BS), BF16),
            pltpu.VMEM((SIDE, nf, tile_rows, LANES), BF16),
            pltpu.VMEM((SLOTS, nf, tile_rows, LANES), BF16),
            pltpu.VMEM(own, BF16),
            pltpu.VMEM(own, BF16),
            pltpu.VMEM((LANES, 256), F32),
            pltpu.VMEM((8 * RW, 8 * RW), BF16),
            pltpu.VMEM((8 * RW, 8 * RW), BF16),
            dma((SLOTS,)), dma((SLOTS,)),
            dma((SLOTS,)), dma((SIDE,)),
            dma((SLOTS,)), dma((SIDE,)),
            dma((SLOTS,)), dma((SIDE,)),
            dma((3, SIDE)), dma((3, SIDE)),
            dma((3, SIDE)), dma((3, SIDE)),
            dma((SIDE,)), dma((SLOTS,)),
            dma((SIDE,)), dma((SLOTS,)),
            dma((SIDE,)), dma((SLOTS,)),
            dma((SLOTS,)), dma((SLOTS,)),
        ],
        compiler_params=pltpu.CompilerParams(
            collective_id=0, has_side_effects=True, vmem_limit_bytes=40 * 1024 * 1024
        ),
    )(tiles, assignment, extents.reshape(-1), root_left, root_right)
    new_left = BETA * factor_left + left_term.astype(F32)
    new_right = BETA * factor_right + right_term.astype(F32)
    line = jnp.arange(nblocks, dtype=jnp.int32)
    places = (line % SLOTS) * nf + line // SLOTS
    inverse = jnp.sum(jnp.where(assignment[None, :] == line[:, None], places[None, :], 0), axis=1)
    flat = ret.reshape(nblocks, BS // LANES, rpf, LANES).transpose(0, 2, 1, 3).reshape(nblocks, rpf, BS)
    update = flat.at[inverse].get(mode="promise_in_bounds").reshape(nblocks, 1, rpf, BS)
    return (update, new_left, new_right)


def solution(mesh):
    placed = (
        P(None, "rep", "fsdp", None),
        P(),
        P(),
        P("fsdp", "rep", None),
        P("fsdp", "rep", None),
        P("fsdp", "rep", None),
        P("fsdp", "rep", None),
    )
    return jax.shard_map(
        functools.partial(local, mesh.shape["fsdp"]),
        mesh=mesh,
        in_specs=placed,
        out_specs=(P(None, "rep", "fsdp", None), P("fsdp", "rep", None), P("fsdp", "rep", None)),
        check_vma=False,
    )
```

time: 485 us -> 93.4 us (0.19)
  waiting for transfers between devices: 402 us -> 0 us
  Pallas kernels: 0 us -> 83.2 us
  starting transfers between devices: 31 us -> 0 us
  matrix products: 24.8 us -> 0 us
  between operations: 14.4 us -> 0.74 us
  other arithmetic: 6.49 us -> 1.53 us
    all_gather x6 -> x0, waiting for transfers between devices: 349 us -> none  [the longest x3 179 us: local(): precond_full = lax.all_gather(precond_part, 'rep', axis=2, tiled=True)]
    pallas_call x0 -> x1, Pallas kernels: none -> 83.2 us  [local(): pl.pallas_call(functools.partial(kernel, nf), out_shape=(jax.ShapeDtypeSt...]
    all_to_all x2 -> x0, waiting for transfers between devices: 51.7 us -> none  [the longest x1 26.7 us: local(): lax.all_to_all(ordered, 'fsdp', split_axis=0, concat_axis=2, tiled=True)]
    all_to_all x2 -> x0, starting transfers between devices: 30.7 us -> none  [the longest x1 16.9 us: local(): lax.all_to_all(ordered, 'fsdp', split_axis=0, concat_axis=2, tiled=True)]
    dot_general x12 -> x0, matrix products: 24.8 us -> none  [the longest x3 9.03 us: factor_terms(): jnp.einsum('kad,kid->kai', gathered, root_r, preferred_element_type=jnp.f...]
  transfers between devices with their start and end apart: 8 -> 0, of which waited for: 8 -> 0; matrix products, arithmetic and copies ran while one was open for 5% -> 0% of each run, Pallas kernels for 0% -> 0%
where the time goes in v1:
time: 93.4 us; the launch traced here: 91.8 us
  Pallas kernels  83.2 us (89%)
  local copies, waits for them, and re-layouts  6.35 us (7%)
  other arithmetic  1.53 us (2%)
    pallas_call x1, Pallas kernels, local(): pl.pallas_call(functools.partial(kernel, nf), out_shape=(jax.ShapeDtypeSt...  83.2 us
    unnamed x15, local copies, waits for them, and re-layouts  2.44 us
    gather x1, local copies, waits for them, and re-layouts, local(): flat.at[inverse].get(mode='promise_in_bounds').reshape(nblocks, 1, rpf, BS)  2.17 us

profile of v1, /device:TPU:1, one launch (start us, length us, event | category | flops | bytes accessed | tf_op | source)
XLA Modules:
  0.0 91.8 jit_solution(13939528216724447710)
XLA Ops:
  0.6 0.0 copy-start
  0.6 1.0 %copy-done = bf16[96,1,2,1024]{3,2,1,0:T(2,128)(2,1)S(1)} copy-done((bf16[96,1,2,1024]{3,2,1,0:T(2,128)(2,1)S(1)}, bf16[96,1,2,1024]{3,2,1,0:T(2,128)(2,1)}, u32[]{:S(2)}) %copy-start) | copy-done | bytes 393240
  1.6 0.0 copy-start.3
  1.6 0.6 copy-done.3
  2.3 0.1 select_reduce_fusion
  2.4 0.1 reshape.95
  2.5 0.1 copy.15
  2.6 0.1 reshape.96
  2.7 0.0 copy-start.6
  2.7 0.7 copy-done.6
  3.4 0.1 copy.17
  3.5 0.1 reshape.99.ext
  3.6 0.0 copy-start.1
  3.6 0.0 copy-start.2
  3.7 1.4 %gather_fusion = bf16[96,2,1024]{2,1,0:T(2,128)(2,1)S(1)} fusion(bf16[96,2,1024]{2,1,0:T(2,128)(2,1)S(1)} %bitcast.19, s32[1024]{0:T(1024)S(1)} %pad_clamp_fusion.1), kind=kCustom, calls=%fused_computation | custom fusion | bytes 786816 | tf_op jit(solution)/shard_map/gather | solution.py:304
  5.0 0.0 copy-done.1
  5.0 0.0 copy-done.2
  5.0 0.0 copy-start.4
  5.0 83.2 %shard_map.94 = (bf16[3,32,16,128]{3,2,1,0:T(8,128)(2,1)S(1)}, bf16[3,64,1024]{2,1,0:T(8,128)(2,1)S(1)}, bf16[3,64,1024]{2,1,0:T(8,128)(2,1)S(1)}) custom-call(bf16[3,32,16,128]{3,2,1,0:T(8,128)(2,1)S(1)} %bitcast.20, s32[96]{0:T(128)S(1)} %copy-done.3, s32[192]{0:T(256)S(1)} %reshape.99.ext, bf16[3,64,1024]{2,1,0:T(8,128)(2,1)S(1)} %copy-done.1, ...), custom_call_target="tpu_custom_call" | custom-call | tf_op jit(solution)/shard_map/pallas_call | solution.py:313
  88.2 0.0 copy-start.5
  88.3 2.2 %gather_fusion.1 = bf16[96,2,1024]{2,1,0:T(2,128)(2,1)} fusion(bf16[96,2,1024]{2,1,0:T(2,128)(2,1)S(1)} %bitcast.21, s32[1024]{0:T(1024)S(1)} %pad_clamp_fusion), kind=kCustom, calls=%fused_computation.1 | custom fusion | bytes 786816 | tf_op jit(solution)/shard_map/gather | solution.py:359
  90.4 0.0 copy-done.4
  90.4 0.0 copy-done.5
  90.4 1.4 %convert_add_fusion = (f32[3,64,1024]{2,1,0:T(8,128)}, f32[3,64,1024]{2,1,0:T(8,128)}) fusion(bf16[3,64,1024]{2,1,0:T(8,128)(2,1)S(1)} %get-tuple-element.8, f32[3,64,1024]{2,1,0:T(8,128)S(1)} %copy-done.4, bf16[3,64,1024]{2,1,0:T(8,128)(2,1)S(1)} %get-tuple-element.7, f32[3,64,1024]{2,1,0:T(8,128)S(1)} %copy-done.5), kind=kLoop, calls=%fused_computation.2 | loop fusion | flops 1179648 | bytes 3932160 | tf_op jit(solution)/shard_map/add | solution.py:354
  (5 shorter events, 0.0 us)
Async XLA Ops:
  0.6 1.0 %copy-start = (bf16[96,1,2,1024]{3,2,1,0:T(2,128)(2,1)S(1)}, bf16[96,1,2,1024]{3,2,1,0:T(2,128)(2,1)}, u32[]{:S(2)}) copy-start(bf16[96,1,2,1024]{3,2,1,0:T(2,128)(2,1)} %param.7) | copy-start | bytes 1179652
  1.6 0.7 copy-start.3
  2.7 0.7 copy-start.6
  3.6 1.4 %copy-start.1 = (bf16[3,64,1024]{2,1,0:T(8,128)(2,1)S(1)}, bf16[3,64,1024]{2,1,0:T(8,128)(2,1)}, u32[]{:S(2)}) copy-start(bf16[3,64,1024]{2,1,0:T(8,128)(2,1)} %root_l.1) | copy-start | bytes 1179652
  3.6 1.4 %copy-start.2 = (bf16[3,64,1024]{2,1,0:T(8,128)(2,1)S(1)}, bf16[3,64,1024]{2,1,0:T(8,128)(2,1)}, u32[]{:S(2)}) copy-start(bf16[3,64,1024]{2,1,0:T(8,128)(2,1)} %root_r.1) | copy-start | bytes 1179652
  5.0 85.4 %copy-start.4 = (f32[3,64,1024]{2,1,0:T(8,128)S(1)}, f32[3,64,1024]{2,1,0:T(8,128)}, u32[]{:S(2)}) copy-start(f32[3,64,1024]{2,1,0:T(8,128)} %param.11) | copy-start | bytes 2359300
  88.2 2.2 %copy-start.5 = (f32[3,64,1024]{2,1,0:T(8,128)S(1)}, f32[3,64,1024]{2,1,0:T(8,128)}, u32[]{:S(2)}) copy-start(f32[3,64,1024]{2,1,0:T(8,128)} %param.10) | copy-start | bytes 2359300

commit v2 on v1

v2 whole, which is shorter than its diff:
```python
import functools

import jax
import jax.numpy as jnp
from jax import lax
from jax.experimental import pallas as pl
from jax.experimental.pallas import tpu as pltpu
from jax.sharding import PartitionSpec as P

BETA = 0.95
MESH = pl.DeviceIdType.MESH
SIDE = 4
SLOTS = 3
RW = 64
BS = 1024
LANES = 128
F32 = jnp.float32
BF16 = jnp.bfloat16


def kernel(
    nf, grads, asg_in, ext_in, root_l, root_r, ret, left_out, right_out,
    asg, ext, grads_v, tiles, zin, fold_in, g_full, r_full, l_own, g_own, t_buf, u_buf, u_tiles, u_in, left_buf, right_buf, turned, g_cols,
    perm, perm_t,
    grads_sem, asg_sem, ext_sem, z_send, z_recv, gf_send, gf_recv, rf_send, rf_recv, lf_send, lf_recv,
    ga_send, ga_recv, ra_send, ra_recv, u_send, u_recv, lo_send, lo_recv, ro_send, ro_recv, b_send, b_recv,
):
    me = lax.axis_index("fsdp")
    rep = lax.axis_index("rep")
    core = lax.rem(me, 2)
    y, x = rep // SIDE, lax.rem(rep, SIDE)
    fold = jnp.where(core == 0, y, x)
    ring = jnp.where(core == 0, x, y)
    fold_step = jnp.where(core == 0, SIDE, 1)
    ring_step = jnp.where(core == 0, 1, SIDE)

    def at(fold_pos, ring_pos):
        return fold_pos * fold_step + ring_pos * ring_step

    right = lax.rem(ring + 1, SIDE)
    left = lax.rem(ring + SIDE - 1, SIDE)
    across = lax.rem(ring + 2, SIDE)
    works = fold < SLOTS

    def remote(src, dst, ssem, rsem, fs, rp):
        return pltpu.make_async_remote_copy(
            src_ref=src, dst_ref=dst, send_sem=ssem, recv_sem=rsem, device_id=(fs, rp), device_id_type=MESH
        )

    def taken(ref, sem):
        pltpu.make_async_copy(ref, ref, sem).wait()

    staged = pltpu.make_async_copy(grads, grads_v, grads_sem)
    staged.start()
    numbers = pltpu.make_async_copy(asg_in, asg, asg_sem)
    numbers.start()
    limits = pltpu.make_async_copy(ext_in, ext, ext_sem)
    limits.start()

    barrier = pltpu.get_barrier_semaphore()

    def greet(d, carry):
        pl.semaphore_signal(barrier, inc=1, device_id=(lax.rem(me + d, nf), rep), device_id_type=MESH)
        return carry

    for d in range(1, SIDE):
        pl.semaphore_signal(barrier, inc=1, device_id=(me, at(lax.rem(fold + d, SIDE), ring)), device_id_type=MESH)
    for pos in (left, right):
        pl.semaphore_signal(barrier, inc=1, device_id=(me, at(fold, pos)), device_id_type=MESH)
    lax.fori_loop(1, nf, greet, 0)
    pl.semaphore_wait(barrier, nf - 1 + SIDE - 1 + 2)

    def fold_root(root, place, sends, recvs):
        def push(s, carry):
            @pl.when(fold != s)
            def _():
                remote(root.at[s], place, sends.at[s], recvs.at[fold], me, at(s, ring)).start()

            @pl.when(fold == s)
            def _():
                pltpu.make_async_copy(root.at[s], place, recvs.at[fold]).start()

            return carry

        lax.fori_loop(0, SLOTS, push, 0)

    def other(i):
        half = (nf + 1 - i) // 2
        return lax.rem(me + jnp.where(lax.rem(i, 2) == 0, half, nf - half), nf)

    def send_tiles(s, carry):
        def push(i, carry):
            to = other(i)
            tiles[s, to] = grads_v[asg[to * SLOTS + s]]
            remote(tiles.at[s, to], zin.at[s, me], z_send.at[s], z_recv.at[s], to, rep).start()
            return carry

        lax.fori_loop(1, nf, push, 0)
        tiles[s, me] = grads_v[asg[me * SLOTS + s]]
        pltpu.make_async_copy(tiles.at[s, me], zin.at[s, me], z_recv.at[s]).start()
        return carry

    fold_root(root_r, r_full.at[rep], rf_send, rf_recv)
    staged.wait()
    numbers.wait()
    limits.wait()
    lax.fori_loop(0, SLOTS, send_tiles, 0)
    fold_root(root_l, l_own.at[fold], lf_send, lf_recv)

    one = lax.broadcasted_iota(jnp.int32, (LANES, LANES), 0)
    two = lax.broadcasted_iota(jnp.int32, (LANES, LANES), 1)

    def tile_place(o):
        return (lax.rem(o, 16) // 2) * 16 + (o // 16) * 2 + lax.rem(o, 2)

    perm[...] = jnp.where(two == tile_place(one), 1.0, 0.0).astype(BF16)
    perm_t[...] = jnp.where(one == tile_place(two), 1.0, 0.0).astype(BF16)

    def spread(buf, sends, recvs, f):
        g = at(f, ring)
        remote(buf.at[g], buf.at[g], sends.at[0, f], recvs.at[0, f], me, at(fold, right)).start()
        remote(buf.at[g], buf.at[g], sends.at[1, f], recvs.at[1, f], me, at(fold, left)).start()

    def pass_on(buf, sends, recvs):
        def push(i, carry):
            way = lax.rem(i, 2)
            f = way * 2 + i // 2
            g = at(f, jnp.where(way == 0, left, right))
            taken(buf.at[g], recvs.at[way, f])
            to = at(fold, jnp.where(way == 0, right, left))
            remote(buf.at[g], buf.at[g], sends.at[2, f], recvs.at[2, f], me, to).start()
            return carry

        lax.fori_loop(0, SIDE, push, 0)

    def rest(buf, recvs):
        def await_piece(f, carry):
            way = 1 - f // 2
            taken(buf.at[at(f, jnp.where(way == 0, left, right))], recvs.at[way, f])
            taken(buf.at[at(f, across)], recvs.at[2, f])
            return carry

        lax.fori_loop(0, SIDE, await_piece, 0)

    slot = me * SLOTS + jnp.minimum(fold, SLOTS - 1)
    block = asg[slot]
    rows_ok = ext[0, block]
    cols_ok = ext[1, block]

    def unpack(i, carry):
        f = lax.rem(fold + i, SIDE)
        taken(fold_in.at[f], gf_recv.at[f])
        g = at(f, ring)
        groups = [fold_in[f, q * 8 : (q + 1) * 8].reshape(LANES, LANES) for q in range(4)]
        flat = jnp.dot(perm[...], jnp.concatenate(groups, axis=1), preferred_element_type=F32)
        row_ids = g * RW + lax.broadcasted_iota(jnp.int32, (16, LANES), 0)
        col_ids = lax.broadcasted_iota(jnp.int32, (16, LANES), 1)
        for q in range(4):
            for c in range(BS // LANES):
                ok = jnp.logical_and(row_ids + q * 16 < rows_ok, col_ids + c * LANES < cols_ok)
                part = flat[c * 16 : (c + 1) * 16, q * LANES : (q + 1) * LANES]
                part = jnp.where(ok, part, 0.0).astype(BF16)
                g_full[g, q * 16 : (q + 1) * 16, c * LANES : (c + 1) * LANES] = part
                g_own[f, q * 16 : (q + 1) * 16, c * LANES : (c + 1) * LANES] = part
        spread(g_full, ga_send, ga_recv, f)
        return carry

    own_rows = SIDE * RW

    def update_part():
        rest(g_full, ga_recv)

        def await_left(f, carry):
            taken(l_own.at[f], lf_recv.at[f])
            return carry

        lax.fori_loop(0, SIDE, await_left, 0)
        t_buf[...] = jnp.dot(
            l_own[...].reshape(own_rows, BS), g_full[...].reshape(BS, BS), preferred_element_type=F32
        ).astype(BF16)
        rest(r_full, ra_recv)
        u = jnp.dot(t_buf[...], r_full[...].reshape(BS, BS), preferred_element_type=F32)
        col_ids = lax.broadcasted_iota(jnp.int32, (RW, BS), 1)
        for f in range(SIDE):
            row_ids = at(f, ring) * RW + lax.broadcasted_iota(jnp.int32, (RW, BS), 0)
            ok = jnp.logical_and(row_ids < rows_ok, col_ids < cols_ok)
            u_buf[f * RW : (f + 1) * RW, :] = jnp.where(ok, u[f * RW : (f + 1) * RW, :], 0.0).astype(BF16)

        def pack(i, carry):
            f = lax.rem(fold + 1 + i, SIDE)
            rows = u_buf[pl.ds(pl.multiple_of(f * RW, RW), RW), :]
            groups = [
                jnp.concatenate(
                    [rows[q * 16 : (q + 1) * 16, c * LANES : (c + 1) * LANES] for c in range(BS // LANES)], axis=0
                )
                for q in range(4)
            ]
            flat = jnp.dot(perm_t[...], jnp.concatenate(groups, axis=1), preferred_element_type=F32).astype(BF16)
            for q in range(4):
                u_tiles[f, q * 8 : (q + 1) * 8] = flat[:, q * LANES : (q + 1) * LANES].reshape(8, 16, LANES)

            @pl.when(fold != f)
            def _():
                remote(u_tiles.at[f], u_in.at[fold], u_send.at[f], u_recv.at[fold], me, at(f, ring)).start()

            @pl.when(fold == f)
            def _():
                pltpu.make_async_copy(u_tiles.at[f], u_in.at[fold], u_recv.at[fold]).start()

            return carry

        lax.fori_loop(0, SIDE, pack, 0)

    def factor_part():
        part = lax.dot_general(
            g_own[...].reshape(own_rows, BS),
            g_full[...].reshape(BS, BS),
            (((1,), (1,)), ((), ())),
            preferred_element_type=F32,
        )
        left_buf[...] = ((1.0 - BETA) * part).astype(BF16).reshape(SIDE, RW, BS)

        def home(buf, out, sends, recvs, f):
            @pl.when(fold != f)
            def _():
                remote(buf.at[f], out.at[fold], sends.at[f], recvs.at[fold], me, at(f, ring)).start()

            @pl.when(fold == f)
            def _():
                pltpu.make_async_copy(buf.at[f], out.at[fold], recvs.at[fold]).start()

        def left_home(f, carry):
            home(left_buf, left_out, lo_send, lo_recv, f)
            return carry

        lax.fori_loop(0, SIDE, left_home, 0)

        def own_columns(f, carry):
            g = at(f, ring)
            pair = pl.ds(pl.multiple_of((g // 2) * LANES, LANES), LANES)
            turned[...] = g_full[:, :, pair].reshape(BS, LANES).T
            g_cols[f] = turned[pl.ds(pl.multiple_of(lax.rem(g, 2) * RW, RW), RW), :]
            return carry

        lax.fori_loop(0, SIDE, own_columns, 0)
        part = jnp.dot(g_cols[...].reshape(own_rows, BS), g_full[...].reshape(BS, BS), preferred_element_type=F32)
        right_buf[...] = ((1.0 - BETA) * part).astype(BF16).reshape(SIDE, RW, BS)

        def right_home(f, carry):
            home(right_buf, right_out, ro_send, ro_recv, f)
            return carry

        lax.fori_loop(0, SIDE, right_home, 0)

    def send_back(s):
        taken(u_in.at[s], u_recv.at[s])

        def push_back(i, carry):
            to = other(i)
            remote(u_in.at[s, to], ret.at[s, me], b_send.at[s], b_recv.at[s], to, rep).start()
            return carry

        lax.fori_loop(1, nf, push_back, 0)
        pltpu.make_async_copy(u_in.at[s, me], ret.at[s, me], b_recv.at[s]).start()

    @pl.when(works)
    def _():
        def root_piece(f, carry):
            taken(r_full.at[at(f, ring)], rf_recv.at[f])
            spread(r_full, ra_send, ra_recv, f)
            return carry

        lax.fori_loop(0, SIDE, root_piece, 0)

    def fold_tiles(s, carry):
        taken(zin.at[s], z_recv.at[s])

        @pl.when(fold != s)
        def _():
            remote(zin.at[s], fold_in.at[fold], gf_send.at[s], gf_recv.at[fold], me, at(s, ring)).start()

        @pl.when(fold == s)
        def _():
            pltpu.make_async_copy(zin.at[s], fold_in.at[fold], gf_recv.at[fold]).start()
            lax.fori_loop(0, SIDE, unpack, 0)

        @pl.when(jnp.logical_and(works, s == 0))
        def _():
            pass_on(r_full, ra_send, ra_recv)

        return carry

    lax.fori_loop(0, SLOTS, fold_tiles, 0)

    @pl.when(works)
    def _():
        pass_on(g_full, ga_send, ga_recv)

    def turn(s, carry):
        @pl.when(jnp.logical_and(works, s == jnp.maximum(fold - 1, 0)))
        def _():
            update_part()

        send_back(s)
        pl.when(fold == s)(factor_part)
        return carry

    lax.fori_loop(0, SLOTS, turn, 0)

    def finish(s, carry):
        taken(left_out.at[s], lo_recv.at[s])
        taken(right_out.at[s], ro_recv.at[s])
        taken(ret.at[s], b_recv.at[s])
        taken(tiles.at[s, pl.ds(0, nf - 1)], z_send.at[s])
        taken(u_in.at[s, pl.ds(0, nf - 1)], b_send.at[s])

        @pl.when(fold != s)
        def _():
            taken(zin.at[s], gf_send.at[s])
            taken(root_r.at[s], rf_send.at[s])
            taken(root_l.at[s], lf_send.at[s])

        return carry

    lax.fori_loop(0, SLOTS, finish, 0)

    @pl.when(works)
    def _():
        def sent(f, carry):
            for way in range(3):
                taken(g_full.at[f], ga_send.at[way, f])
                taken(r_full.at[f], ra_send.at[way, f])

            @pl.when(fold != f)
            def _():
                taken(u_tiles.at[f], u_send.at[f])
                taken(left_buf.at[f], lo_send.at[f])
                taken(right_buf.at[f], ro_send.at[f])

            return carry

        lax.fori_loop(0, SIDE, sent, 0)


def local(nf, grads, assignment, extents, factor_left, factor_right, root_left, root_right):
    nblocks = assignment.shape[0]
    rpf = RW // nf
    tile_rows = rpf * BS // LANES
    split = grads.reshape(nblocks, rpf, BS // LANES, LANES).transpose(0, 2, 1, 3).reshape(nblocks, tile_rows, LANES)
    dma = pltpu.SemaphoreType.DMA
    anywhere = pl.BlockSpec(memory_space=pl.ANY)
    hbm = pl.BlockSpec(memory_space=pltpu.HBM)
    rows = (SLOTS, RW, BS)
    own = (SIDE, RW, BS)
    ret, left_term, right_term = pl.pallas_call(
        functools.partial(kernel, nf),
        out_shape=(
            jax.ShapeDtypeStruct((SLOTS, nf, tile_rows, LANES), BF16),
            jax.ShapeDtypeStruct(rows, BF16),
            jax.ShapeDtypeStruct(rows, BF16),
        ),
        in_specs=[hbm] * 5,
        out_specs=(anywhere, anywhere, anywhere),
        scratch_shapes=[
            pltpu.SMEM((nblocks,), jnp.int32),
            pltpu.SMEM((2, nblocks), jnp.int32),
            pltpu.VMEM((nblocks, tile_rows, LANES), BF16),
            pltpu.VMEM((SLOTS, nf, tile_rows, LANES), BF16),
            pltpu.VMEM((SLOTS, nf, tile_rows, LANES), BF16),
            pltpu.VMEM((SIDE, nf, tile_rows, LANES), BF16),
            pltpu.VMEM((SIDE * SIDE, RW, BS), BF16),
            pltpu.VMEM((SIDE * SIDE, RW, BS), BF16),
            pltpu.VMEM(own, BF16),
            pltpu.VMEM(own, BF16),
            pltpu.VMEM((SIDE * RW, BS), BF16),
            pltpu.VMEM((SIDE * RW, BS), BF16),
            pltpu.VMEM((SIDE, nf, tile_rows, LANES), BF16),
            pltpu.VMEM((SLOTS, nf, tile_rows, LANES), BF16),
            pltpu.VMEM(own, BF16),
            pltpu.VMEM(own, BF16),
            pltpu.VMEM((LANES, BS), BF16),
            pltpu.VMEM(own, BF16),
            pltpu.VMEM((LANES, LANES), BF16),
            pltpu.VMEM((LANES, LANES), BF16),
            dma, dma, dma,
            dma((SLOTS,)), dma((SLOTS,)),
            dma((SLOTS,)), dma((SIDE,)),
            dma((SLOTS,)), dma((SIDE,)),
            dma((SLOTS,)), dma((SIDE,)),
            dma((3, SIDE)), dma((3, SIDE)),
            dma((3, SIDE)), dma((3, SIDE)),
            dma((SIDE,)), dma((SLOTS,)),
            dma((SIDE,)), dma((SLOTS,)),
            dma((SIDE,)), dma((SLOTS,)),
            dma((SLOTS,)), dma((SLOTS,)),
        ],
        compiler_params=pltpu.CompilerParams(
            collective_id=0, has_side_effects=True, vmem_limit_bytes=60 * 1024 * 1024
        ),
    )(split, assignment, extents.T, root_left, root_right)
    new_left = BETA * factor_left + left_term.astype(F32)
    new_right = BETA * factor_right + right_term.astype(F32)
    line = jnp.arange(nblocks, dtype=jnp.int32)
    places = (line % SLOTS) * nf + line // SLOTS
    inverse = jnp.sum(jnp.where(assignment[None, :] == line[:, None], places[None, :], 0), axis=1)
    flat = ret.reshape(nblocks, BS // LANES, rpf, LANES).transpose(0, 2, 1, 3).reshape(nblocks, rpf, BS)
    update = flat.at[inverse].get(mode="promise_in_bounds").reshape(nblocks, 1, rpf, BS)
    return (update, new_left, new_right)


def solution(mesh):
    placed = (
        P(None, "rep", "fsdp", None),
        P(),
        P(),
        P("fsdp", "rep", None),
        P("fsdp", "rep", None),
        P("fsdp", "rep", None),
        P("fsdp", "rep", None),
    )
    return jax.shard_map(
        functools.partial(local, mesh.shape["fsdp"]),
        mesh=mesh,
        in_specs=placed,
        out_specs=(P(None, "rep", "fsdp", None), P("fsdp", "rep", None), P("fsdp", "rep", None)),
        check_vma=False,
    )
```

time: 93.4 us -> 81.7 us (0.87)
  Pallas kernels: 83.2 us -> 73.9 us
  local copies, waits for them, and re-layouts: 6.35 us -> 3.87 us
  other arithmetic: 1.53 us -> 2.49 us
    pallas_call x1, Pallas kernels: 83.2 us -> 73.9 us  [local(): pl.pallas_call(functools.partial(kernel, nf), out_shape=(jax.ShapeDtypeSt...]
    unnamed x15 -> x8, local copies, waits for them, and re-layouts: 2.44 us -> 0.65 us
    gather x1 -> x0, local copies, waits for them, and re-layouts: 1.36 us -> none  [local(): grads.reshape(nblocks, rpf, BS).at[by_slot].get(mode='promise_in_bounds')]
    gather x1, local copies, waits for them, and re-layouts: 2.17 us -> 3.22 us  [local(): flat.at[inverse].get(mode='promise_in_bounds').reshape(nblocks, 1, rpf, BS)]
    add x1, other arithmetic: 1.38 us -> 2.36 us  [local(): new_right = BETA * factor_right + right_term.astype(F32)]
where the time goes in v2:
time: 81.7 us; the launch traced here: 81 us
  Pallas kernels  73.9 us (90%)
  local copies, waits for them, and re-layouts  3.87 us (5%)
  other arithmetic  2.49 us (3%)
    pallas_call x1, Pallas kernels, local(): pl.pallas_call(functools.partial(kernel, nf), out_shape=(jax.ShapeDtypeSt...  73.9 us
    gather x1, local copies, waits for them, and re-layouts, local(): flat.at[inverse].get(mode='promise_in_bounds').reshape(nblocks, 1, rpf, BS)  3.22 us
    add x1, other arithmetic, local(): new_right = BETA * factor_right + right_term.astype(F32)  2.36 us

profile of v2, /device:TPU:1, one launch (start us, length us, event | category | flops | bytes accessed | tf_op | source)
XLA Modules:
  0.0 81.0 jit_solution(15928312500517600081)
XLA Ops:
  0.6 0.0 copy-start.3
  0.7 0.6 copy-done.3
  1.3 0.1 select_reduce_fusion
  1.4 0.0 copy-start
  1.4 0.0 copy-start.1
  1.4 73.9 %shard_map.94 = (bf16[3,32,16,128]{3,2,1,0:T(8,128)(2,1)}, bf16[3,64,1024]{2,1,0:T(8,128)(2,1)}, bf16[3,64,1024]{2,1,0:T(8,128)(2,1)}) custom-call(bf16[96,16,128]{2,1,0:T(8,128)(2,1)} %bitcast.16, s32[96]{0:T(128)} %asg_in.1, s32[2,96]{1,0:T(2,128)} %bitcast.19, bf16[3,64,1024]{2,1,0:T(8,128)(2,1)} %root_l.1, bf16[3,64,1024]{2,1,0:T(8,128)(2,1)} %root_r.1), custom_call_target="tpu_custom_call" | custom-call | tf_op jit(solution)/shard_map/pallas_call | solution.py:355
  75.4 0.0 copy-start.2
  75.4 3.2 %gather_fusion = bf16[96,2,1024]{2,1,0:T(2,128)(2,1)} fusion(bf16[96,2,1024]{2,1,0:T(2,128)(2,1)} %bitcast.18, s32[1024]{0:T(1024)S(1)} %pad_clamp_fusion), kind=kCustom, calls=%fused_computation | custom fusion | bytes 786816 | tf_op jit(solution)/shard_map/gather | solution.py:407
  78.6 0.0 copy-done
  78.6 0.0 copy-done.1
  78.6 0.0 copy-done.2
  78.6 2.4 %convert_add_fusion = (f32[3,64,1024]{2,1,0:T(8,128)}, f32[3,64,1024]{2,1,0:T(8,128)}) fusion(bf16[3,64,1024]{2,1,0:T(8,128)(2,1)} %get-tuple-element.8, f32[3,64,1024]{2,1,0:T(8,128)S(1)} %copy-done, bf16[3,64,1024]{2,1,0:T(8,128)(2,1)S(1)} %copy-done.2, f32[3,64,1024]{2,1,0:T(8,128)S(1)} %copy-done.1), kind=kLoop, calls=%fused_computation.1 | loop fusion | flops 1179648 | bytes 3932160 | tf_op jit(solution)/shard_map/add | solution.py:402
  (3 shorter events, 0.0 us)
Async XLA Ops:
  0.6 0.7 copy-start.3
  1.4 77.2 %copy-start = (f32[3,64,1024]{2,1,0:T(8,128)S(1)}, f32[3,64,1024]{2,1,0:T(8,128)}, u32[]{:S(2)}) copy-start(f32[3,64,1024]{2,1,0:T(8,128)} %param.11) | copy-start | bytes 2359300
  1.4 77.2 %copy-start.1 = (f32[3,64,1024]{2,1,0:T(8,128)S(1)}, f32[3,64,1024]{2,1,0:T(8,128)}, u32[]{:S(2)}) copy-start(f32[3,64,1024]{2,1,0:T(8,128)} %param.10) | copy-start | bytes 2359300
  75.4 3.2 %copy-start.2 = (bf16[3,64,1024]{2,1,0:T(8,128)(2,1)S(1)}, bf16[3,64,1024]{2,1,0:T(8,128)(2,1)}, u32[]{:S(2)}) copy-start(bf16[3,64,1024]{2,1,0:T(8,128)(2,1)} %get-tuple-element.7) | copy-start | bytes 1179652

commit v3 on v2

--- a/solution.py
+++ b/solution.py
@@ -19,10 +19,10 @@
 
 
 def kernel(
-    nf, grads, asg_in, ext_in, root_l, root_r, ret, left_out, right_out,
-    asg, ext, grads_v, tiles, zin, fold_in, g_full, r_full, l_own, g_own, t_buf, u_buf, u_tiles, u_in, left_buf, right_buf, turned, g_cols,
+    nf, grads, asg_in, ext_in, places_in, root_l, root_r, left_in, right_in, update_out, new_left, new_right,
+    asg, ext, places, ret, left_out, right_out, factor_l, factor_r, grads_v, tiles, zin, fold_in, g_full, r_full, l_own, g_own, t_buf, u_buf, u_tiles, u_in, left_buf, right_buf, turned, g_cols,
     perm, perm_t,
-    grads_sem, asg_sem, ext_sem, z_send, z_recv, gf_send, gf_recv, rf_send, rf_recv, lf_send, lf_recv,
+    grads_sem, asg_sem, ext_sem, places_sem, factor_sem, z_send, z_recv, gf_send, gf_recv, rf_send, rf_recv, lf_send, lf_recv,
     ga_send, ga_recv, ra_send, ra_recv, u_send, u_recv, lo_send, lo_recv, ro_send, ro_recv, b_send, b_recv,
 ):
     me = lax.axis_index("fsdp")
@@ -56,6 +56,8 @@
     numbers.start()
     limits = pltpu.make_async_copy(ext_in, ext, ext_sem)
     limits.start()
+    order = pltpu.make_async_copy(places_in, places, places_sem)
+    order.start()
 
     barrier = pltpu.get_barrier_semaphore()
 
@@ -104,8 +106,16 @@
     staged.wait()
     numbers.wait()
     limits.wait()
+    order.wait()
     lax.fori_loop(0, SLOTS, send_tiles, 0)
     fold_root(root_l, l_own.at[fold], lf_send, lf_recv)
+
+    factors = [
+        pltpu.make_async_copy(left_in, factor_l, factor_sem.at[0]),
+        pltpu.make_async_copy(right_in, factor_r, factor_sem.at[1]),
+    ]
+    for copy in factors:
+        copy.start()
 
     one = lax.broadcasted_iota(jnp.int32, (LANES, LANES), 0)
     two = lax.broadcasted_iota(jnp.int32, (LANES, LANES), 1)
@@ -307,10 +317,32 @@
 
     lax.fori_loop(0, SLOTS, turn, 0)
 
+    for copy in factors:
+        copy.wait()
+
+    def new_factors(s, carry):
+        taken(left_out.at[s], lo_recv.at[s])
+        new_left[s] = BETA * factor_l[s] + left_out[s].astype(F32)
+        taken(right_out.at[s], ro_recv.at[s])
+        new_right[s] = BETA * factor_r[s] + right_out[s].astype(F32)
+        return carry
+
+    lax.fori_loop(0, SLOTS, new_factors, 0)
+
+    def returned(s, carry):
+        taken(ret.at[s], b_recv.at[s])
+        return carry
+
+    lax.fori_loop(0, SLOTS, returned, 0)
+
+    def block_order(b, carry):
+        place = places[b]
+        update_out[b] = ret[place // nf, lax.rem(place, nf)]
+        return carry
+
+    lax.fori_loop(0, nf * SLOTS, block_order, 0, unroll=4)
+
     def finish(s, carry):
-        taken(left_out.at[s], lo_recv.at[s])
-        taken(right_out.at[s], ro_recv.at[s])
-        taken(ret.at[s], b_recv.at[s])
         taken(tiles.at[s, pl.ds(0, nf - 1)], z_send.at[s])
         taken(u_in.at[s, pl.ds(0, nf - 1)], b_send.at[s])
 
@@ -341,29 +373,37 @@
 
         lax.fori_loop(0, SIDE, sent, 0)
 
-
 def local(nf, grads, assignment, extents, factor_left, factor_right, root_left, root_right):
     nblocks = assignment.shape[0]
     rpf = RW // nf
     tile_rows = rpf * BS // LANES
     split = grads.reshape(nblocks, rpf, BS // LANES, LANES).transpose(0, 2, 1, 3).reshape(nblocks, tile_rows, LANES)
     dma = pltpu.SemaphoreType.DMA
-    anywhere = pl.BlockSpec(memory_space=pl.ANY)
+    vmem = pl.BlockSpec(memory_space=pltpu.VMEM)
     hbm = pl.BlockSpec(memory_space=pltpu.HBM)
     rows = (SLOTS, RW, BS)
     own = (SIDE, RW, BS)
-    ret, left_term, right_term = pl.pallas_call(
+    line = jnp.arange(nblocks, dtype=jnp.int32)
+    slot_places = (line % SLOTS) * nf + line // SLOTS
+    places = jnp.sum(jnp.where(assignment[None, :] == line[:, None], slot_places[None, :], 0), axis=1)
+    update, new_left, new_right = pl.pallas_call(
         functools.partial(kernel, nf),
         out_shape=(
-            jax.ShapeDtypeStruct((SLOTS, nf, tile_rows, LANES), BF16),
-            jax.ShapeDtypeStruct(rows, BF16),
-            jax.ShapeDtypeStruct(rows, BF16),
+            pltpu.VMEM((nblocks, tile_rows, LANES), BF16),
+            pltpu.VMEM(rows, F32),
+            pltpu.VMEM(rows, F32),
         ),
-        in_specs=[hbm] * 5,
-        out_specs=(anywhere, anywhere, anywhere),
+        in_specs=[hbm] * 8,
+        out_specs=(vmem, vmem, vmem),
         scratch_shapes=[
             pltpu.SMEM((nblocks,), jnp.int32),
             pltpu.SMEM((2, nblocks), jnp.int32),
+            pltpu.SMEM((nblocks,), jnp.int32),
+            pltpu.VMEM((SLOTS, nf, tile_rows, LANES), BF16),
+            pltpu.VMEM(rows, BF16),
+            pltpu.VMEM(rows, BF16),
+            pltpu.VMEM(rows, F32),
+            pltpu.VMEM(rows, F32),
             pltpu.VMEM((nblocks, tile_rows, LANES), BF16),
             pltpu.VMEM((SLOTS, nf, tile_rows, LANES), BF16),
             pltpu.VMEM((SLOTS, nf, tile_rows, LANES), BF16),
@@ -382,7 +422,8 @@
             pltpu.VMEM(own, BF16),
             pltpu.VMEM((LANES, LANES), BF16),
             pltpu.VMEM((LANES, LANES), BF16),
-            dma, dma, dma,
+            dma, dma, dma, dma,
+            dma((2,)),
             dma((SLOTS,)), dma((SLOTS,)),
             dma((SLOTS,)), dma((SIDE,)),
             dma((SLOTS,)), dma((SIDE,)),
@@ -395,16 +436,10 @@
             dma((SLOTS,)), dma((SLOTS,)),
         ],
         compiler_params=pltpu.CompilerParams(
-            collective_id=0, has_side_effects=True, vmem_limit_bytes=60 * 1024 * 1024
+            collective_id=0, has_side_effects=True, vmem_limit_bytes=56 * 1024 * 1024
         ),
-    )(split, assignment, extents.T, root_left, root_right)
-    new_left = BETA * factor_left + left_term.astype(F32)
-    new_right = BETA * factor_right + right_term.astype(F32)
-    line = jnp.arange(nblocks, dtype=jnp.int32)
-    places = (line % SLOTS) * nf + line // SLOTS
-    inverse = jnp.sum(jnp.where(assignment[None, :] == line[:, None], places[None, :], 0), axis=1)
-    flat = ret.reshape(nblocks, BS // LANES, rpf, LANES).transpose(0, 2, 1, 3).reshape(nblocks, rpf, BS)
-    update = flat.at[inverse].get(mode="promise_in_bounds").reshape(nblocks, 1, rpf, BS)
+    )(split, assignment, extents.T, places, root_left, root_right, factor_left, factor_right)
+    update = update.reshape(nblocks, BS // LANES, rpf, LANES).transpose(0, 2, 1, 3).reshape(nblocks, 1, rpf, BS)
     return (update, new_left, new_right)
 
 

time: 81.7 us -> 79.4 us (0.972)
  other arithmetic: 2.49 us -> 0.64 us
    gather x1 -> x0, local copies, waits for them, and re-layouts: 3.22 us -> none  [local(): flat.at[inverse].get(mode='promise_in_bounds').reshape(nblocks, 1, rpf, BS)]
    unnamed x8 -> x5, local copies, waits for them, and re-layouts: 0.65 us -> 3.14 us
    add x2 -> x1, other arithmetic: 2.38 us -> 0.01 us  [local(): slot_places = line % SLOTS * nf + line // SLOTS]
where the time goes in v3:
time: 79.4 us; the launch traced here: 78.9 us
  Pallas kernels  74.4 us (94%)
  local copies, waits for them, and re-layouts  3.14 us (4%)
    pallas_call x1, Pallas kernels, local(): pl.pallas_call(functools.partial(kernel, nf), out_shape=(pltpu.VMEM((nblo...  74.4 us
    unnamed x5, local copies, waits for them, and re-layouts  3.14 us

profile of v3, /device:TPU:1, one launch (start us, length us, event | category | flops | bytes accessed | tf_op | source)
XLA Modules:
  0.0 78.9 jit_solution(1954926214215653345)
XLA Ops:
  0.6 0.0 copy-start
  0.7 0.6 copy-done
  1.3 0.6 select_reduce_fusion.places_in
  1.9 74.4 %shard_map.94 = (bf16[96,16,128]{2,1,0:T(8,128)(2,1)S(1)}, f32[3,64,1024]{2,1,0:T(8,128)S(1)}, f32[3,64,1024]{2,1,0:T(8,128)S(1)}) custom-call(bf16[96,16,128]{2,1,0:T(8,128)(2,1)} %bitcast.12, s32[96]{0:T(128)} %asg_in.1, s32[2,96]{1,0:T(2,128)} %bitcast.13, s32[96]{0:T(128)} %select_reduce_fusion.places_in, bf16[3,64,1024]{2,1,0:T(8,128)(2,1)} %root_l.1, ...), custom_call_target="tpu_custom_call" | custom-call | tf_op jit(solution)/shard_map/pallas_call | solution.py:389
  76.3 0.7 copy.17
  77.1 0.9 %copy.18 = f32[3,64,1024]{2,1,0:T(8,128)} copy(f32[3,64,1024]{2,1,0:T(8,128)S(1)} %get-tuple-element.10) | data formatting | bytes 1572864
  78.0 0.9 %copy.19 = f32[3,64,1024]{2,1,0:T(8,128)} copy(f32[3,64,1024]{2,1,0:T(8,128)S(1)} %get-tuple-element.11) | data formatting | bytes 1572864
  (1 shorter events, 0.0 us)
Async XLA Ops:
  0.6 0.7 copy-start

commit v4 on v3

--- a/solution.py
+++ b/solution.py
@@ -19,8 +19,8 @@
 
 
 def kernel(
-    nf, grads, asg_in, ext_in, places_in, root_l, root_r, left_in, right_in, update_out, new_left, new_right,
-    asg, ext, places, ret, left_out, right_out, factor_l, factor_r, grads_v, tiles, zin, fold_in, g_full, r_full, l_own, g_own, t_buf, u_buf, u_tiles, u_in, left_buf, right_buf, turned, g_cols,
+    nf, grads, asg_in, ext_in, root_l, root_r, left_in, right_in, update_out, new_left, new_right,
+    asg, ext, places, places_v, ret, left_out, right_out, factor_l, factor_r, grads_v, tiles, zin, fold_in, g_full, r_full, l_own, g_own, t_buf, u_buf, u_tiles, u_in, left_buf, right_buf, turned, g_cols,
     perm, perm_t,
     grads_sem, asg_sem, ext_sem, places_sem, factor_sem, z_send, z_recv, gf_send, gf_recv, rf_send, rf_recv, lf_send, lf_recv,
     ga_send, ga_recv, ra_send, ra_recv, u_send, u_recv, lo_send, lo_recv, ro_send, ro_recv, b_send, b_recv,
@@ -56,8 +56,6 @@
     numbers.start()
     limits = pltpu.make_async_copy(ext_in, ext, ext_sem)
     limits.start()
-    order = pltpu.make_async_copy(places_in, places, places_sem)
-    order.start()
 
     barrier = pltpu.get_barrier_semaphore()
 
@@ -106,7 +104,6 @@
     staged.wait()
     numbers.wait()
     limits.wait()
-    order.wait()
     lax.fori_loop(0, SLOTS, send_tiles, 0)
     fold_root(root_l, l_own.at[fold], lf_send, lf_recv)
 
@@ -282,6 +279,15 @@
 
         lax.fori_loop(0, SIDE, root_piece, 0)
 
+    lanes = lax.broadcasted_iota(jnp.int32, (8, LANES), 1)
+
+    def place_of(k, found):
+        return jnp.where(lanes == asg[k], lax.rem(k, SLOTS) * nf + k // SLOTS, found)
+
+    places_v[...] = lax.fori_loop(0, nf * SLOTS, place_of, jnp.zeros((8, LANES), jnp.int32))
+    order = pltpu.make_async_copy(places_v, places, places_sem)
+    order.start()
+
     def fold_tiles(s, carry):
         taken(zin.at[s], z_recv.at[s])
 
@@ -335,8 +341,10 @@
 
     lax.fori_loop(0, SLOTS, returned, 0)
 
+    order.wait()
+
     def block_order(b, carry):
-        place = places[b]
+        place = places[0, b]
         update_out[b] = ret[place // nf, lax.rem(place, nf)]
         return carry
 
@@ -383,9 +391,6 @@
     hbm = pl.BlockSpec(memory_space=pltpu.HBM)
     rows = (SLOTS, RW, BS)
     own = (SIDE, RW, BS)
-    line = jnp.arange(nblocks, dtype=jnp.int32)
-    slot_places = (line % SLOTS) * nf + line // SLOTS
-    places = jnp.sum(jnp.where(assignment[None, :] == line[:, None], slot_places[None, :], 0), axis=1)
     update, new_left, new_right = pl.pallas_call(
         functools.partial(kernel, nf),
         out_shape=(
@@ -393,12 +398,13 @@
             pltpu.VMEM(rows, F32),
             pltpu.VMEM(rows, F32),
         ),
-        in_specs=[hbm] * 8,
+        in_specs=[hbm] * 7,
         out_specs=(vmem, vmem, vmem),
         scratch_shapes=[
             pltpu.SMEM((nblocks,), jnp.int32),
             pltpu.SMEM((2, nblocks), jnp.int32),
-            pltpu.SMEM((nblocks,), jnp.int32),
+            pltpu.SMEM((8, LANES), jnp.int32),
+            pltpu.VMEM((8, LANES), jnp.int32),
             pltpu.VMEM((SLOTS, nf, tile_rows, LANES), BF16),
             pltpu.VMEM(rows, BF16),
             pltpu.VMEM(rows, BF16),
@@ -438,7 +444,7 @@
         compiler_params=pltpu.CompilerParams(
             collective_id=0, has_side_effects=True, vmem_limit_bytes=56 * 1024 * 1024
         ),
-    )(split, assignment, extents.T, places, root_left, root_right, factor_left, factor_right)
+    )(split, assignment, extents.T, root_left, root_right, factor_left, factor_right)
     update = update.reshape(nblocks, BS // LANES, rpf, LANES).transpose(0, 2, 1, 3).reshape(nblocks, 1, rpf, BS)
     return (update, new_left, new_right)
 

time: 79.4 us -> 78.2 us (0.985)
    unnamed x5 -> x3, local copies, waits for them, and re-layouts: 3.14 us -> 2.51 us
where the time goes in v4:
time: 78.2 us; the launch traced here: 77.7 us
  Pallas kernels  74.5 us (95%)
  local copies, waits for them, and re-layouts  2.51 us (3%)
    pallas_call x1, Pallas kernels, local(): pl.pallas_call(functools.partial(kernel, nf), out_shape=(pltpu.VMEM((nblo...  74.5 us
    unnamed x3, local copies, waits for them, and re-layouts  2.51 us

profile of v4, /device:TPU:1, one launch (start us, length us, event | category | flops | bytes accessed | tf_op | source)
XLA Modules:
  0.0 77.7 jit_solution(12063240600190422730)
XLA Ops:
  0.6 74.5 %shard_map.94 = (bf16[96,16,128]{2,1,0:T(8,128)(2,1)S(1)}, f32[3,64,1024]{2,1,0:T(8,128)S(1)}, f32[3,64,1024]{2,1,0:T(8,128)S(1)}) custom-call(bf16[96,16,128]{2,1,0:T(8,128)(2,1)} %bitcast.12, s32[96]{0:T(128)} %asg_in.1, s32[2,96]{1,0:T(2,128)} %bitcast.13, bf16[3,64,1024]{2,1,0:T(8,128)(2,1)} %root_l.1, bf16[3,64,1024]{2,1,0:T(8,128)(2,1)} %root_r.1, ...), custom_call_target="tpu_custom_call" | custom-call | tf_op jit(solution)/shard_map/pallas_call | solution.py:394
  75.2 0.7 copy.15
  75.9 0.9 %copy.16 = f32[3,64,1024]{2,1,0:T(8,128)} copy(f32[3,64,1024]{2,1,0:T(8,128)S(1)} %get-tuple-element.10) | data formatting | bytes 1572864
  76.8 0.9 %copy.17 = f32[3,64,1024]{2,1,0:T(8,128)} copy(f32[3,64,1024]{2,1,0:T(8,128)S(1)} %get-tuple-element.11) | data formatting | bytes 1572864
